TPU v7x, 256 devices: a whole 4x4x8 slice. The times are simulated.
256 devices in a mesh: sec: 2 (over z_hi), grp: 16 (over x, z_lo), tp: 8 (over y, core).
Axes of the slice: x: 4, y: 4, z: 8 (z_hi: 2, z_lo: 4; z = z_hi * 4 + z_lo), core: 2. Of those that a mesh axis runs over, the one named last changes fastest.
Arguments:
- pre_query: bfloat16 [32, 1024, 8192], P(('sec', 'grp'), 'tp'), may hold values from -6 to 6
- pre_keys: bfloat16 [32, 2048, 1024], P(('sec', 'grp'), 'tp'), may hold values from -6 to 6
- pre_values: bfloat16 [32, 2048, 1024], P(('sec', 'grp'), 'tp'), may hold values from -6 to 6
- dec_query: bfloat16 [32, 2, 64, 8192], P(('sec', 'grp'), None, None, 'tp'), may hold values from -6 to 6
- dec_new_keys: bfloat16 [32, 2, 64, 1024], P(('sec', 'grp'), None, None, 'tp'), may hold values from -6 to 6
- dec_new_values: bfloat16 [32, 2, 64, 1024], P(('sec', 'grp'), None, None, 'tp'), may hold values from -6 to 6
- cache_keys: bfloat16 [32, 64, 16, 1024], P(('sec', 'grp'), None, None, 'tp'), may hold values from -6 to 6
- cache_values: bfloat16 [32, 64, 16, 1024], P(('sec', 'grp'), None, None, 'tp'), may hold values from -6 to 6
- cache_lens: int32 [32, 64], P(('sec', 'grp')), may hold values from 1 to 16
- pool_keys: bfloat16 [32, 8, 32, 16, 1024], P(('sec', 'grp'), 'tp'), may hold values from -6 to 6
- pool_values: bfloat16 [32, 8, 32, 16, 1024], P(('sec', 'grp'), 'tp'), may hold values from -6 to 6
- block_owner: int32 [32, 8, 32, 1], P(('sec', 'grp'), 'tp'), may hold values from 0 to 31; in each aligned block of 32 rows (0 to 31, 32 to 63, ..., all dimensions but the last counted through in order) at most 2 rows name the same one
- block_count: int32 [32, 8, 32], P(('sec', 'grp'), 'tp'), may hold values from 1 to 16
Outputs:
- pre_out: bfloat16 [32, 1024, 8192], P(('sec', 'grp'), 'tp')
- dec_out: bfloat16 [32, 2, 64, 8192], P(('sec', 'grp'), None, None, 'tp')
- pages_keys: bfloat16 [32, 32, 8, 2, 16, 1024], P(('sec', 'grp'), None, None, None, None, 'tp')
- pages_values: bfloat16 [32, 32, 8, 2, 16, 1024], P(('sec', 'grp'), None, None, None, None, 'tp')
Inputs may be any that keep to these rules, and one draw needn't show every extreme that they name: `block_owner`: no owner is named by more than 2 of the blocks of one device, and some device names some owner exactly 2 times.
All inputs are finite; a program needn't handle non-finite values.
Results may differ from a plain program's by a relative error of at most 0.0085.
Values may be sent and summed in bfloat16 or wider, within the bound.
A program may use at most 192 MiB of HBM per device.

v0:
```python
import jax
import jax.numpy as jnp
from jax import lax
from jax.sharding import PartitionSpec as P

H = 64
KVH = 8
HD = 128
CAP = 2


MASKED_SCORE = -1e30


def prefill_part(pre_query, pre_keys, pre_values):
    queries = pre_query[0]
    span_dev = queries.shape[0]
    key_dev = pre_keys.shape[1]
    tp_count = lax.axis_size("tp")
    prior_len = (key_dev - span_dev) * tp_count
    groups = H // KVH
    scaling = HD ** (-0.5)
    first_pos = prior_len + lax.axis_index("tp") * span_dev
    query_pos = first_pos + jnp.arange(span_dev, dtype=jnp.int32)
    last_pos = first_pos + span_dev - 1
    grouped = queries.reshape(span_dev, KVH, groups, HD)
    initial = (
        jnp.full((span_dev, KVH, groups), MASKED_SCORE, jnp.float32),
        jnp.zeros((span_dev, KVH, groups), jnp.float32),
        jnp.zeros((span_dev, KVH, groups, HD), jnp.float32),
    )
    key_rows = lax.all_gather(pre_keys[0], "tp", axis=0, tiled=True)
    value_rows = lax.all_gather(pre_values[0], "tp", axis=0, tiled=True)
    length = key_rows.shape[0]
    key_pos = jnp.arange(length, dtype=jnp.int32)
    allowed = (key_pos[None, :] <= query_pos[:, None])[:, None, None, :]

    def update(state):
        row_max, denominator, accum = state
        scores = (
            jnp.einsum(
                "qkgd,tkd->qkgt",
                grouped,
                key_rows.reshape(length, KVH, HD),
                preferred_element_type=jnp.float32,
            )
            * scaling
        )
        scores = jnp.where(allowed, scores, MASKED_SCORE)
        new_max = jnp.maximum(row_max, jnp.max(scores, axis=-1))
        weights = jnp.where(allowed, jnp.exp(scores - new_max[..., None]), 0.0)
        denominator = jnp.sum(weights, axis=-1)
        partial_sum = jnp.einsum(
            "qkgt,tkd->qkgd",
            weights.astype(jnp.bfloat16),
            value_rows.reshape(length, KVH, HD),
            preferred_element_type=jnp.float32,
        )
        accum = partial_sum
        return (new_max, denominator, accum)

    row_max, denominator, accum = lax.cond(
        jnp.int32(0) <= last_pos, update, lambda state: state, initial
    )
    result = accum / denominator[..., None]
    return result.reshape(1, span_dev, H * HD).astype(jnp.bfloat16)


def decode_part(dec_query, dec_new_keys, dec_new_values, cache_keys, cache_values, cache_lens):
    groups = H // KVH
    scaling = HD ** (-0.5)
    steps_count = dec_query.shape[1]
    row_count = dec_query.shape[2]
    local_kv = dec_new_keys.shape[3] // HD
    cache_len = cache_keys.shape[2]
    grouped = dec_query[0].reshape(steps_count, row_count, local_kv, groups, HD)
    cache_k = cache_keys[0].reshape(row_count, cache_len, local_kv, HD)
    cache_v = cache_values[0].reshape(row_count, cache_len, local_kv, HD)
    fresh_k = dec_new_keys[0].reshape(steps_count, row_count, local_kv, HD)
    fresh_v = dec_new_values[0].reshape(steps_count, row_count, local_kv, HD)
    lengths = cache_lens[0]
    cache_scores = (
        jnp.einsum("sbkgd,bckd->sbkgc", grouped, cache_k, preferred_element_type=jnp.float32)
        * scaling
    )
    fresh_scores = (
        jnp.einsum("sbkgd,ubkd->sbkgu", grouped, fresh_k, preferred_element_type=jnp.float32)
        * scaling
    )
    cache_ok = (jnp.arange(cache_len, dtype=jnp.int32)[None, :] < lengths[:, None])[
        None, :, None, None, :
    ]
    step_ids = jnp.arange(steps_count, dtype=jnp.int32)
    fresh_ok = (step_ids[None, :] <= step_ids[:, None])[:, None, None, None, :]
    cache_scores = jnp.where(cache_ok, cache_scores, MASKED_SCORE)
    fresh_scores = jnp.where(fresh_ok, fresh_scores, MASKED_SCORE)
    row_max = jnp.maximum(jnp.max(cache_scores, axis=-1), jnp.max(fresh_scores, axis=-1))[..., None]
    cache_weights = jnp.where(cache_ok, jnp.exp(cache_scores - row_max), 0.0)
    fresh_weights = jnp.where(fresh_ok, jnp.exp(fresh_scores - row_max), 0.0)
    denominator = jnp.sum(cache_weights, axis=-1) + jnp.sum(fresh_weights, axis=-1)
    mixture = jnp.einsum(
        "sbkgc,bckd->sbkgd",
        cache_weights.astype(jnp.bfloat16),
        cache_v,
        preferred_element_type=jnp.float32,
    )
    mixture = mixture + jnp.einsum(
        "sbkgu,ubkd->sbkgd",
        fresh_weights.astype(jnp.bfloat16),
        fresh_v,
        preferred_element_type=jnp.float32,
    )
    result = mixture / denominator[..., None]
    return result.reshape(1, steps_count, row_count, local_kv * groups * HD).astype(jnp.bfloat16)


def handoff_part(pool_keys, pool_values, block_owner, block_count):
    replicas = lax.axis_size(("sec", "grp"))
    tp_count = lax.axis_size("tp")
    owners = block_owner[0, 0, :, 0]
    counts = block_count[0, 0]
    pool_len = owners.shape[0]
    block_len = pool_keys.shape[3]
    width = pool_keys.shape[4]
    slice_width = width // tp_count
    onehot = (owners[:, None] == jnp.arange(replicas, dtype=jnp.int32)[None, :]).astype(jnp.int32)
    slot_index = jnp.sum((jnp.cumsum(onehot, axis=0) - 1) * onehot, axis=1)
    target_rep = jnp.arange(replicas * CAP, dtype=jnp.int32) // CAP
    target_slot = jnp.arange(replicas * CAP, dtype=jnp.int32) % CAP
    selector = (
        (owners[None, :] == target_rep[:, None]) & (slot_index[None, :] == target_slot[:, None])
    ).astype(jnp.bfloat16)
    usable = (jnp.arange(block_len, dtype=jnp.int32)[None, :] < counts[:, None])[:, :, None]

    def pack(pool):
        masked = jnp.where(usable, pool[0, 0], jnp.zeros((), pool.dtype)).reshape(
            pool_len, block_len * width
        )
        packed = jnp.dot(selector, masked, preferred_element_type=jnp.float32).astype(jnp.bfloat16)
        return packed.reshape(replicas, 1, CAP, block_len, tp_count, slice_width)

    send_keys = pack(pool_keys)
    send_values = pack(pool_values)
    got_keys, got_values = (
        lax.all_to_all(
            lax.all_to_all(send_keys, ("sec", "grp"), split_axis=0, concat_axis=0, tiled=True),
            "tp",
            split_axis=4,
            concat_axis=1,
            tiled=True,
        ),
        lax.all_to_all(
            lax.all_to_all(send_values, ("sec", "grp"), split_axis=0, concat_axis=0, tiled=True),
            "tp",
            split_axis=4,
            concat_axis=1,
            tiled=True,
        ),
    )
    out_shape = (1, replicas, tp_count, CAP, block_len, slice_width)
    return (got_keys.reshape(out_shape), got_values.reshape(out_shape))


def body(
    pre_query,
    pre_keys,
    pre_values,
    dec_query,
    dec_new_keys,
    dec_new_values,
    cache_keys,
    cache_values,
    cache_lens,
    pool_keys,
    pool_values,
    block_owner,
    block_count,
):
    pages_keys, pages_values = handoff_part(pool_keys, pool_values, block_owner, block_count)
    dec_out = decode_part(
        dec_query, dec_new_keys, dec_new_values, cache_keys, cache_values, cache_lens
    )
    pre_out = prefill_part(pre_query, pre_keys, pre_values)
    return (pre_out, dec_out, pages_keys, pages_values)


def solution(mesh):
    return jax.shard_map(
        body,
        mesh=mesh,
        in_specs=(
            P(("sec", "grp"), "tp", None),
            P(("sec", "grp"), "tp", None),
            P(("sec", "grp"), "tp", None),
            P(("sec", "grp"), None, None, "tp"),
            P(("sec", "grp"), None, None, "tp"),
            P(("sec", "grp"), None, None, "tp"),
            P(("sec", "grp"), None, None, "tp"),
            P(("sec", "grp"), None, None, "tp"),
            P(("sec", "grp"), None),
            P(("sec", "grp"), "tp", None, None, None),
            P(("sec", "grp"), "tp", None, None, None),
            P(("sec", "grp"), "tp", None, None),
            P(("sec", "grp"), "tp", None),
        ),
        out_specs=(
            P(("sec", "grp"), "tp", None),
            P(("sec", "grp"), None, None, "tp"),
            P(("sec", "grp"), None, None, None, None, "tp"),
            P(("sec", "grp"), None, None, None, None, "tp"),
        ),
        check_vma=False,
    )
```

profile of v0, /device:TPU:48, one launch (start us, length us, event | category | flops | bytes accessed | tf_op | source)
XLA Modules:
  0.0 298.4 jit_solution(17040727771243382488)
XLA Ops:
  7.9 0.7 iota_compare_fusion.1
  9.4 1.8 copy.67
  11.5 0.8 fusion.18
  12.8 1.8 copy.40
  14.6 11.2 %all-to-all-start = ((bf16[32,1,2,16,8,128]{5,3,2,4,1,0:T(8,128)(2,1)}), bf16[32,1,2,16,8,128]{5,3,2,4,1,0:T(8,128)(2,1)S(1)}, u32[]{:S(2)}, u32[]{:S(2)}) async-start(bf16[32,1,2,16,8,128]{5,3,2,4,1,0:T(8,128)(2,1)} %copy.40), calls=%async_computation | async-start | bytes 4194304 | tf_op jit(solution)/shard_map/all_to_all | solution.py:146
  25.8 1.8 copy.69
  27.7 0.7 fusion.19
  29.0 1.8 copy.42
  30.8 44.7 %all-to-all-done = bf16[32,1,2,16,8,128]{5,3,2,4,1,0:T(8,128)(2,1)S(1)} async-done(((bf16[32,1,2,16,8,128]{5,3,2,4,1,0:T(8,128)(2,1)}), bf16[32,1,2,16,8,128]{5,3,2,4,1,0:T(8,128)(2,1)S(1)}, u32[]{:S(2)}, u32[]{:S(2)}) %all-to-all-start) | async-done | bytes 2097184 | tf_op jit(solution)/shard_map/all_to_all | solution.py:146
  75.5 6.1 %all-to-all-start.2 = ((bf16[32,1,2,16,8,128]{5,3,2,4,1,0:T(8,128)(2,1)}), bf16[32,1,2,16,8,128]{5,3,2,4,1,0:T(8,128)(2,1)}, u32[]{:S(2)}, u32[]{:S(2)}) async-start(bf16[32,1,2,16,8,128]{5,3,2,4,1,0:T(8,128)(2,1)} %copy.42), calls=%async_computation.2 | async-start | bytes 4194304 | tf_op jit(solution)/shard_map/all_to_all | solution.py:153
  81.6 0.7 all-gather.7.cloned.1.call-update
  82.3 1.8 copy.41
  84.1 47.4 %all-to-all-done.2 = bf16[32,1,2,16,8,128]{5,3,2,4,1,0:T(8,128)(2,1)} async-done(((bf16[32,1,2,16,8,128]{5,3,2,4,1,0:T(8,128)(2,1)}), bf16[32,1,2,16,8,128]{5,3,2,4,1,0:T(8,128)(2,1)}, u32[]{:S(2)}, u32[]{:S(2)}) %all-to-all-start.2) | async-done | bytes 2097184 | tf_op jit(solution)/shard_map/all_to_all | solution.py:153
  131.4 4.8 %all-to-all-start.1 = ((bf16[32,1,2,16,8,128]{5,3,2,0,1,4:T(8,128)(2,1)}), bf16[32,1,2,16,8,128]{5,3,2,0,1,4:T(8,128)(2,1)S(1)}, u32[]{:S(2)}, u32[]{:S(2)}) async-start(bf16[32,1,2,16,8,128]{5,3,2,0,1,4:T(8,128)(2,1)} %copy.41), calls=%async_computation.1 | async-start | bytes 4194304 | tf_op jit(solution)/shard_map/all_to_all | solution.py:145
  136.3 3.4 %copy.43 = bf16[32,1,2,16,8,128]{5,3,2,0,1,4:T(8,128)(2,1)} copy(bf16[32,1,2,16,8,128]{5,3,2,4,1,0:T(8,128)(2,1)} %all-to-all-done.2) | data formatting | bytes 4194304 | tf_op jit(solution)/shard_map/all_to_all | solution.py:153
  139.7 20.6 %all-to-all-done.1 = bf16[32,1,2,16,8,128]{5,3,2,0,1,4:T(8,128)(2,1)S(1)} async-done(((bf16[32,1,2,16,8,128]{5,3,2,0,1,4:T(8,128)(2,1)}), bf16[32,1,2,16,8,128]{5,3,2,0,1,4:T(8,128)(2,1)S(1)}, u32[]{:S(2)}, u32[]{:S(2)}) %all-to-all-start.1) | async-done | bytes 2097184 | tf_op jit(solution)/shard_map/all_to_all | solution.py:145
  160.3 7.4 %all-to-all-start.3 = ((bf16[32,1,2,16,8,128]{5,3,2,0,1,4:T(8,128)(2,1)}), bf16[32,1,2,16,8,128]{5,3,2,0,1,4:T(8,128)(2,1)}, u32[]{:S(2)}, u32[]{:S(2)}) async-start(bf16[32,1,2,16,8,128]{5,3,2,0,1,4:T(8,128)(2,1)} %copy.43), calls=%async_computation.3 | async-start | bytes 4194304 | tf_op jit(solution)/shard_map/all_to_all | solution.py:152
  167.9 1.3 fusion.63
  171.2 0.8 copy.44
  171.9 1.9 copy.45
  173.9 17.9 %all-to-all-done.3 = bf16[32,1,2,16,8,128]{5,3,2,0,1,4:T(8,128)(2,1)} async-done(((bf16[32,1,2,16,8,128]{5,3,2,0,1,4:T(8,128)(2,1)}), bf16[32,1,2,16,8,128]{5,3,2,0,1,4:T(8,128)(2,1)}, u32[]{:S(2)}, u32[]{:S(2)}) %all-to-all-start.3) | async-done | bytes 2097184 | tf_op jit(solution)/shard_map/all_to_all | solution.py:152
  191.8 3.5 %copy.46 = bf16[1,32,8,2,16,128]{5,4,3,2,1,0:T(8,128)(2,1)} copy(bf16[1,32,8,2,16,128]{5,4,3,1,2,0:T(8,128)(2,1)} %bitcast.35) | data formatting | bytes 4194304
  195.4 89.6 %conditional.1 = (f32[128,8,8]{0,2,1:T(8,128)S(1)}, f32[128,8,8,128]{3,0,2,1:T(8,128)}) conditional(s32[]{:T(128)} %convert_element_type.51, () %tuple.19, (s32[]{:T(128)}, s32[128,1]{0,1:T(1,128)S(1)}, s32[128,1,1,2048]{0,3,2,1:T(8,128)S(1)}, bf16[2048,1024]{1,0:T(8,128)(2,1)}, bf16[1,128,8192]{2,1,0:T(8,128)(2,1)}, ...), branch_computations={%region_0.0_spmd, %region_1.0_spmd} | conditional | flops 8808292352 | bytes 256050752 | solution.py:62
  195.6 2.3 copy.63
  198.3 3.1 %copy.62 = bf16[256,8,8,128]{3,2,1,0:T(8,128)(2,1)} copy(bf16[256,8,8,128]{3,1,2,0:T(8,128)(2,1)S(1)} %bitcast.147) | data formatting | bytes 8388608 | tf_op jit(solution)/shard_map/cond
  201.3 26.4 %fusion = (f32[128,8,8]{0,2,1:T(8,128)S(1)}, f32[8,2048,128,8]{2,1,3,0:T(8,128)}) fusion(pred[128,2048]{0,1:T(8,128)(4,1)S(1)} %compare_bitcast_fusion, bf16[128,8,8,128]{3,2,1,0:T(8,128)(2,1)S(1)} %bitcast.138, bf16[2048,8,128,1]{2,1,0,3:T(8,128)(2,1)} %bitcast.137), kind=kOutput, calls=%fused_computation.2 | convolution fusion | flops 4345290752 | bytes 73695232 | tf_op jit(solution)/shard_map/cond/branch_1_fun/qkgd,tkd->qkgt/dot_general | solution.py:41
  227.8 21.5 %fusion.2 = f32[128,8,8]{0,2,1:T(8,128)S(1)} fusion(f32[8,2048,128,8]{2,1,3,0:T(8,128)} %get-tuple-element.57, f32[128,8,8]{0,2,1:T(8,128)S(1)} %broadcast_maximum_fusion, pred[128,2048]{0,1:T(8,128)(4,1)S(1)} %compare_bitcast_fusion), kind=kLoop, calls=%fused_computation.4 | loop fusion | flops 83877888 | bytes 67436544 | tf_op jit(solution)/shard_map/cond/branch_1_fun/reduce_sum | solution.py:52
  249.2 5.3 %copy.64 = bf16[256,8,8,128]{3,2,1,0:T(8,128)(2,1)} copy(bf16[256,8,8,128]{3,1,2,0:T(8,128)(2,1)} %bitcast.149) | data formatting | bytes 8388608 | tf_op jit(solution)/shard_map/cond
  254.5 30.5 %fusion.9 = f32[128,8,8,128]{3,0,2,1:T(8,128)} fusion(bf16[2048,8,128,1]{2,1,0,3:T(8,128)(2,1)} %bitcast.150, f32[8,2048,128,8]{2,1,3,0:T(8,128)} %get-tuple-element.57, f32[128,8,8]{0,2,1:T(8,128)S(1)} %broadcast_maximum_fusion, pred[128,2048]{0,1:T(8,128)(4,1)S(1)} %compare_bitcast_fusion), kind=kOutput, calls=%fused_computation.10 | convolution fusion | flops 4378853376 | bytes 75792384 | tf_op jit(solution)/shard_map/cond/branch_1_fun/qkgt,tkd->qkgd/dot_general | solution.py:53
  285.0 2.9 divide_convert_fusion
  287.9 1.4 copy.35
  289.3 2.3 convert_element_type.53
  (47 shorter events, 5.6 us)
Async XLA Ops:
  7.2 163.2 %copy-start = (bf16[1,64,16,128]{3,2,1,0:T(8,128)(2,1)S(1)}, bf16[1,64,16,128]{3,2,1,0:T(8,128)(2,1)}, u32[]{:S(2)}) copy-start(bf16[1,64,16,128]{3,2,1,0:T(8,128)(2,1)} %param.22) | copy-start | bytes 786436
  7.2 4.0 %copy-start.5 = (s32[1,1,32,1]{2,3,1,0:T(1,128)S(1)}, s32[1,1,32,1]{2,3,1,0:T(1,128)}, u32[]{:S(2)}) copy-start(s32[1,1,32,1]{2,3,1,0:T(1,128)} %param.26) | copy-start | bytes 388
  7.2 188.2 %all-gather.5.cloned.1.call-start = ((), (), s32[]{:S(2)}) async-start(), calls=%async_computation.4 | async-start | bytes 4718592 | tf_op jit(solution)/shard_map/all_gather | solution.py:32
  14.6 60.8 %all-to-all-start = ((bf16[32,1,2,16,8,128]{5,3,2,4,1,0:T(8,128)(2,1)}), bf16[32,1,2,16,8,128]{5,3,2,4,1,0:T(8,128)(2,1)S(1)}, u32[]{:S(2)}, u32[]{:S(2)}) async-start(bf16[32,1,2,16,8,128]{5,3,2,4,1,0:T(8,128)(2,1)} %copy.40), calls=%async_computation | async-start | bytes 4194304 | tf_op jit(solution)/shard_map/all_to_all | solution.py:146
  75.5 56.0 %all-to-all-start.2 = ((bf16[32,1,2,16,8,128]{5,3,2,4,1,0:T(8,128)(2,1)}), bf16[32,1,2,16,8,128]{5,3,2,4,1,0:T(8,128)(2,1)}, u32[]{:S(2)}, u32[]{:S(2)}) async-start(bf16[32,1,2,16,8,128]{5,3,2,4,1,0:T(8,128)(2,1)} %copy.42), calls=%async_computation.2 | async-start | bytes 4194304 | tf_op jit(solution)/shard_map/all_to_all | solution.py:153
  81.5 113.8 %all-gather.7.cloned.1.call-start = ((), (), s32[]{:S(2)}) async-start(), calls=%async_computation.5 | async-start | bytes 4718592 | tf_op jit(solution)/shard_map/all_gather | solution.py:33
  131.4 28.8 %all-to-all-start.1 = ((bf16[32,1,2,16,8,128]{5,3,2,0,1,4:T(8,128)(2,1)}), bf16[32,1,2,16,8,128]{5,3,2,0,1,4:T(8,128)(2,1)S(1)}, u32[]{:S(2)}, u32[]{:S(2)}) async-start(bf16[32,1,2,16,8,128]{5,3,2,0,1,4:T(8,128)(2,1)} %copy.41), calls=%async_computation.1 | async-start | bytes 4194304 | tf_op jit(solution)/shard_map/all_to_all | solution.py:145
  136.2 31.5 %copy-start.4 = (bf16[1,2,64,1024]{3,2,1,0:T(8,128)(2,1)S(1)}, bf16[1,2,64,1024]{3,2,1,0:T(8,128)(2,1)}, u32[]{:S(2)}) copy-start(bf16[1,2,64,1024]{3,2,1,0:T(8,128)(2,1)} %param.18) | copy-start | bytes 786436
  136.2 31.5 %copy-start.6 = (s32[1,64]{1,0:T(1,128)S(1)}, s32[1,64]{1,0:T(1,128)}, u32[]{:S(2)}) copy-start(s32[1,64]{1,0:T(1,128)} %param.23) | copy-start | bytes 772
  136.2 31.6 %copy-start.7 = (bf16[1,2,64,128]{3,2,1,0:T(8,128)(2,1)S(1)}, bf16[1,2,64,128]{3,2,1,0:T(8,128)(2,1)}, u32[]{:S(2)}) copy-start(bf16[1,2,64,128]{3,2,1,0:T(8,128)(2,1)} %param.19) | copy-start | bytes 98308
  136.3 32.9 %copy-start.3 = (bf16[1,64,16,128]{3,2,1,0:T(8,128)(2,1)S(1)}, bf16[1,64,16,128]{3,2,1,0:T(8,128)(2,1)}, u32[]{:S(2)}) copy-start(bf16[1,64,16,128]{3,2,1,0:T(8,128)(2,1)} %param.21) | copy-start | bytes 786436
  160.3 31.5 %all-to-all-start.3 = ((bf16[32,1,2,16,8,128]{5,3,2,0,1,4:T(8,128)(2,1)}), bf16[32,1,2,16,8,128]{5,3,2,0,1,4:T(8,128)(2,1)}, u32[]{:S(2)}, u32[]{:S(2)}) async-start(bf16[32,1,2,16,8,128]{5,3,2,0,1,4:T(8,128)(2,1)} %copy.43), calls=%async_computation.3 | async-start | bytes 4194304 | tf_op jit(solution)/shard_map/all_to_all | solution.py:152
  167.7 3.0 %copy-start.8 = (bf16[1,2,64,128]{3,2,1,0:T(8,128)(2,1)S(1)}, bf16[1,2,64,128]{3,2,1,0:T(8,128)(2,1)}, u32[]{:S(2)}) copy-start(bf16[1,2,64,128]{3,2,1,0:T(8,128)(2,1)} %param.20) | copy-start | bytes 98308
  195.4 2.8 copy-start.2
  285.0 6.6 %copy-start.1 = (bf16[1,64,16,128]{3,2,1,0:T(8,128)(2,1)S(1)}, bf16[1,64,16,128]{3,2,1,0:T(8,128)(2,1)}, u32[]{:S(2)}) copy-start(bf16[1,64,16,128]{3,2,1,0:T(8,128)(2,1)} %param.22) | copy-start | bytes 786436
Sparse Core Ops, SparseCore 0:
  9.9 35.7 all-gather.4
  84.3 34.4 all-gather.6
where the time goes:
time: 303 us; the launch traced here: 298 us
  waiting for transfers between devices  132 us (44%)
  matrix products  60.8 us (20%)
  local copies, waits for them, and re-layouts  35.3 us (12%)
  starting transfers between devices  29.5 us (10%)
  other arithmetic  26.4 us (9%)
  between operations  14.3 us (5%)
    all_to_all x1, waiting for transfers between devices, handoff_part(): lax.all_to_all(send_values, ('sec', 'grp'), split_axis=0, concat_axis=0,...  47.4 us
    all_to_all x1, waiting for transfers between devices, handoff_part(): lax.all_to_all(send_keys, ('sec', 'grp'), split_axis=0, concat_axis=0, ti...  44.7 us
    dot_general x1, matrix products, update(): jnp.einsum('qkgt,tkd->qkgd', weights.astype(jnp.bfloat16), value_rows.res...  30.5 us
    dot_general x1, matrix products, update(): jnp.einsum('qkgd,tkd->qkgt', grouped, key_rows.reshape(length, KVH, HD),...  26.4 us
    reduce_sum x1, other arithmetic, update(): denominator = jnp.sum(weights, axis=-1)  21.5 us
    all_to_all x1, waiting for transfers between devices, handoff_part(): lax.all_to_all(lax.all_to_all(send_keys, ('sec', 'grp'), split_axis=0, co...  20.6 us
    all_to_all x1, waiting for transfers between devices, handoff_part(): lax.all_to_all(lax.all_to_all(send_values, ('sec', 'grp'), split_axis=0,...  17.9 us
    unnamed x25, local copies, waits for them, and re-layouts  11.6 us
  transfers between devices with their start and end apart: 6, of which 4 were waited for; matrix products, arithmetic and copies ran while one was open for 9% of the time, Pallas kernels for 0%

commit v1 on v0

v1 whole, which is shorter than its diff:
```python
import jax
import jax.numpy as jnp
from jax import lax
from jax.experimental import pallas as pl
from jax.experimental.pallas import tpu as pltpu
from jax.sharding import PartitionSpec as P

H = 64
KVH = 8
HD = 128
G = 8
CAP = 2
BLOCK = 16
REPS = 32
NTP = 8
SPAN_DEV = 128
KEY_DEV = 256
CHIP_KEYS = 2 * KEY_DEV
PRIOR = 1024
ROWS = 64
STEPS = 2
CACHE = 16
UNITS = REPS * NTP
ROW_TILE = 256
LOG2E_SCALE = 1.4426950408889634 * HD**-0.5
MASKED = -1e30
MESH = pl.DeviceIdType.MESH


def position():
    sec, grp, tp = lax.axis_index("sec"), lax.axis_index("grp"), lax.axis_index("tp")
    return grp // 4, tp // 2, sec * 4 + lax.rem(grp, 4), lax.rem(tp, 2)


def replica_at(x, z):
    return z // 4, x * 4 + lax.rem(z, 4)


def kernel(
    table,
    lens,
    pre_q,
    pre_k,
    pre_v,
    dec_q,
    new_k,
    new_v,
    cache_k,
    cache_v,
    pool_k,
    pool_v,
    pre_out,
    dec_out,
    pages,
    qbuf,
    kbuf,
    vbuf,
    poolbuf,
    sendbuf,
    top,
    total,
    accum,
    obuf,
    dqbuf,
    nbuf,
    cbuf,
    dobuf,
    ready,
    load_sem,
    own_sem,
    kv_send,
    kv_relay,
    kv_recv,
    page_send,
    page_recv,
    store_sem,
):
    x, y, z, core = position()
    sec, grp, tp = lax.axis_index("sec"), lax.axis_index("grp"), lax.axis_index("tp")
    me = (sec * 16 + grp) * NTP + tp
    other = y * 2 + 1 - core

    def shifted(k):
        return replica_at(lax.rem(x + k // 8, 4), lax.rem(z + lax.rem(k, 8), 8))

    def sibling(k):
        return lax.rem(tp + k, NTP)

    loads = [
        pltpu.make_async_copy(pool_k.at[0, 0], poolbuf.at[0], load_sem.at[0]),
        pltpu.make_async_copy(pool_v.at[0, 0], poolbuf.at[1], load_sem.at[1]),
        pltpu.make_async_copy(dec_q.at[0], dqbuf, load_sem.at[2]),
        pltpu.make_async_copy(new_k.at[0], nbuf.at[0], load_sem.at[3]),
        pltpu.make_async_copy(new_v.at[0], nbuf.at[1], load_sem.at[4]),
        pltpu.make_async_copy(cache_k.at[0], cbuf.at[0], load_sem.at[5]),
        pltpu.make_async_copy(cache_v.at[0], cbuf.at[1], load_sem.at[6]),
        pltpu.make_async_copy(pre_q.at[0], qbuf, load_sem.at[7]),
    ]
    own_k = pltpu.make_async_copy(pre_k.at[0], kbuf.at[tp], own_sem.at[0])
    own_v = pltpu.make_async_copy(pre_v.at[0], vbuf.at[tp], own_sem.at[1])

    barrier = pltpu.get_barrier_semaphore()

    def greet_replicas(k, _):
        s, g = shifted(k)
        pl.semaphore_signal(barrier, inc=1, device_id=(s, g, tp), device_id_type=MESH)
        return 0

    def greet_siblings(k, _):
        pl.semaphore_signal(barrier, inc=1, device_id=(sec, grp, sibling(k)), device_id_type=MESH)
        return 0

    lax.fori_loop(1, REPS, greet_replicas, 0)
    lax.fori_loop(1, NTP, greet_siblings, 0)
    for copy in loads:
        copy.start()
    own_k.start()
    own_v.start()
    pl.semaphore_wait(barrier, REPS - 1 + NTP - 1)

    def vouch(k, _):
        pl.semaphore_signal(ready, inc=1, device_id=(sec, grp, sibling(k)), device_id_type=MESH)
        return 0

    lax.fori_loop(1, NTP, vouch, 0)

    def chip_at(j):
        return lax.rem(y + jnp.where(j == 0, 0, jnp.where(j == 1, 1, jnp.where(j == 2, 3, 2))), 4)

    def uses(holder, user):
        return jnp.logical_or(holder < 3, user >= 2)

    def kv_direct(j, kv):
        source = (pre_k, pre_v)[kv]
        buf = (kbuf, vbuf)[kv]
        peer = other if j == 0 else chip_at(j) * 2 + core
        return pltpu.make_async_remote_copy(
            src_ref=source.at[0],
            dst_ref=buf.at[tp],
            send_sem=kv_send.at[kv, j],
            recv_sem=kv_recv.at[kv, tp],
            device_id=(sec, grp, peer),
            device_id_type=MESH,
        )

    def kv_relayed(yy, kv):
        buf = (kbuf, vbuf)[kv]
        chunk = yy * 2 + core
        return pltpu.make_async_remote_copy(
            src_ref=buf.at[chunk],
            dst_ref=buf.at[chunk],
            send_sem=kv_relay.at[kv, yy],
            recv_sem=kv_recv.at[kv, chunk],
            device_id=(sec, grp, other),
            device_id_type=MESH,
        )

    def kv_arrival(chunk, kv):
        buf = (kbuf, vbuf)[kv]
        return pltpu.make_async_copy(buf.at[chunk], buf.at[chunk], kv_recv.at[kv, chunk])

    for j in (1, 2, 3, 0):
        @pl.when(uses(y, chip_at(j)))
        def _():
            kv_direct(j, 0).start()
            kv_direct(j, 1).start()

    pl.semaphore_wait(ready, NTP - 1)
    loads[0].wait()
    loads[1].wait()
    token = lax.broadcasted_iota(jnp.int32, (BLOCK, KVH * HD), 0)

    def pack(owner):
        for slot in range(CAP):
            block = table[0, owner * CAP + slot]
            live = table[1, owner * CAP + slot]
            keep = token < live
            for kv in range(2):
                rows = poolbuf[kv, block]
                rows = jnp.where(keep, rows, jnp.zeros_like(rows))
                for t in range(NTP):
                    sendbuf[owner * NTP + t, kv * CAP + slot] = rows[:, t * HD : (t + 1) * HD]

    def page_copy(s, g, t):
        return pltpu.make_async_remote_copy(
            src_ref=sendbuf.at[(s * 16 + g) * NTP + t],
            dst_ref=pages.at[me],
            send_sem=page_send,
            recv_sem=page_recv,
            device_id=(s, g, t),
            device_id_type=MESH,
        )

    def hand_off(k, _):
        s, g = shifted(k)
        pack(s * 16 + g)
        for i in range(NTP):
            page_copy(s, g, sibling(i)).start()
        return 0

    lax.fori_loop(1, REPS, hand_off, 0)
    pack(sec * 16 + grp)
    for i in range(1, NTP):
        page_copy(sec, grp, sibling(i)).start()
    pltpu.make_async_copy(sendbuf.at[me], pages.at[me], page_recv).start()

    for copy in loads[2:]:
        copy.wait()
    shape = (STEPS * G * 16, 16 * CACHE)
    row = lax.broadcasted_iota(jnp.int32, shape, 0)
    col = lax.broadcasted_iota(jnp.int32, shape, 1)
    same_row = lax.rem(row, 16) == col // CACHE
    slot_of = lax.rem(col, CACHE)
    shape = (STEPS * G * 16, STEPS * 16)
    row = lax.broadcasted_iota(jnp.int32, shape, 0)
    col = lax.broadcasted_iota(jnp.int32, shape, 1)
    fresh_ok = jnp.logical_and(lax.rem(row, 16) == lax.rem(col, 16), col // 16 <= row // (G * 16))
    over_d = (((1,), (1,)), ((), ()))

    def decode(i, _):
        rows = pl.ds(pl.multiple_of(i * 16, 16), 16)
        query = jnp.concatenate(
            [dqbuf[s, rows, h * HD : (h + 1) * HD] for s in range(STEPS) for h in range(G)], axis=0
        )
        res_k = cbuf[0, rows].reshape(16 * CACHE, HD)
        res_v = cbuf[1, rows].reshape(16 * CACHE, HD)
        fresh_k = jnp.concatenate([nbuf[0, s, rows] for s in range(STEPS)], axis=0)
        fresh_v = jnp.concatenate([nbuf[1, s, rows] for s in range(STEPS)], axis=0)
        s1 = lax.dot_general(query, res_k, over_d, preferred_element_type=jnp.float32)
        s2 = lax.dot_general(query, fresh_k, over_d, preferred_element_type=jnp.float32)
        ok = jnp.logical_and(same_row, slot_of < lens[i])
        s1 = jnp.where(ok, s1 * LOG2E_SCALE, MASKED)
        s2 = jnp.where(fresh_ok, s2 * LOG2E_SCALE, MASKED)
        peak = jnp.maximum(jnp.max(s1, axis=1, keepdims=True), jnp.max(s2, axis=1, keepdims=True))
        p1 = jnp.exp2(s1 - peak)
        p2 = jnp.exp2(s2 - peak)
        mass = jnp.sum(p1, axis=1, keepdims=True) + jnp.sum(p2, axis=1, keepdims=True)
        out = jnp.dot(p1.astype(jnp.bfloat16), res_v, preferred_element_type=jnp.float32)
        out = out + jnp.dot(p2.astype(jnp.bfloat16), fresh_v, preferred_element_type=jnp.float32)
        out = (out / mass).astype(jnp.bfloat16)
        for s in range(STEPS):
            for h in range(G):
                part = (s * G + h) * 16
                dobuf[s, rows, h * HD : (h + 1) * HD] = out[part : part + 16]
        return 0

    lax.fori_loop(0, ROWS // 16, decode, 0)
    dec_store = pltpu.make_async_copy(dobuf, dec_out.at[0], store_sem.at[0])
    dec_store.start()

    top[...] = jnp.full_like(top, MASKED)
    total[...] = jnp.zeros_like(total)
    accum[...] = jnp.zeros_like(accum)
    shape = (ROW_TILE, CHIP_KEYS)
    ahead = lax.broadcasted_iota(jnp.int32, shape, 1) - lax.rem(
        lax.broadcasted_iota(jnp.int32, shape, 0), SPAN_DEV
    )
    ones = jnp.ones((CHIP_KEYS, HD), jnp.bfloat16)

    def attend(yy):
        reach = PRIOR + SPAN_DEV * tp - CHIP_KEYS * yy
        allowed = ahead <= reach

        def head(g, _):
            lanes = pl.ds(pl.multiple_of(g * HD, HD), HD)
            keys = kbuf[pl.ds(yy * 2, 2), :, lanes].reshape(CHIP_KEYS, HD)
            values = vbuf[pl.ds(yy * 2, 2), :, lanes].reshape(CHIP_KEYS, HD)
            values = jnp.concatenate([values, ones], axis=1)
            for part in range(G * SPAN_DEV // ROW_TILE):
                where = pl.ds(part * ROW_TILE, ROW_TILE)
                heads = ROW_TILE // SPAN_DEV
                query = jnp.concatenate(
                    [
                        qbuf[:, pl.ds(pl.multiple_of((g * G + part * heads + h) * HD, HD), HD)]
                        for h in range(heads)
                    ],
                    axis=0,
                )
                s = lax.dot_general(query, keys, over_d, preferred_element_type=jnp.float32)
                s = jnp.where(allowed, s * LOG2E_SCALE, MASKED)
                old = top[g, where]
                new = jnp.maximum(old, jnp.max(s, axis=1, keepdims=True))
                top[g, where] = new
                weights = jnp.exp2(s - jnp.concatenate([new] * (CHIP_KEYS // HD), axis=1))
                mix = jnp.dot(weights.astype(jnp.bfloat16), values, preferred_element_type=jnp.float32)
                fade = jnp.exp2(old - new)
                accum[g, where] = accum[g, where] * fade + mix[:, :HD]
                total[g, where] = total[g, where] * fade + mix[:, HD:]
            return 0

        lax.fori_loop(0, KVH, head, 0)

    own_k.wait()
    own_v.wait()

    def step(j, _):
        here = chip_at(j)
        later = chip_at(j + 1)

        @pl.when(jnp.logical_and(j < 3, uses(later, y)))
        def _():
            for kv in range(2):
                kv_arrival(later * 2 + core, kv).wait()
                kv_relayed(later, kv).start()

        @pl.when(uses(here, y))
        def _():
            for kv in range(2):
                kv_arrival(here * 2 + 1 - core, kv).wait()
            attend(here)

        return 0

    lax.fori_loop(0, 4, step, 0)

    def finish(g, _):
        for h in range(G):
            where = pl.ds(h * SPAN_DEV, SPAN_DEV)
            lanes = pl.ds(pl.multiple_of((g * G + h) * HD, HD), HD)
            obuf[:, lanes] = (accum[g, where] / total[g, where]).astype(jnp.bfloat16)
        return 0

    lax.fori_loop(0, KVH, finish, 0)
    pre_store = pltpu.make_async_copy(obuf, pre_out.at[0], store_sem.at[1])
    pre_store.start()

    for j in range(4):
        @pl.when(uses(y, chip_at(j)))
        def _():
            kv_direct(j, 0).wait_send()
            kv_direct(j, 1).wait_send()

    for j in range(1, 4):
        @pl.when(uses(chip_at(j), y))
        def _():
            kv_relayed(chip_at(j), 0).wait_send()
            kv_relayed(chip_at(j), 1).wait_send()

    dec_store.wait()
    pre_store.wait()
    some = pl.ds(0, UNITS - 1)
    pltpu.make_async_copy(sendbuf.at[some], sendbuf.at[some], page_send).wait()
    pltpu.make_async_copy(pages, pages, page_recv).wait()


def block_table(owners, counts):
    blocks = jnp.arange(owners.shape[0], dtype=jnp.int32)
    earlier = (owners[None, :] == owners[:, None]) & (blocks[None, :] < blocks[:, None])
    slot = jnp.sum(earlier.astype(jnp.int32), axis=1)
    place = owners * CAP + slot
    chosen = place[None, :] == jnp.arange(REPS * CAP, dtype=jnp.int32)[:, None]
    pair = jnp.stack([blocks, counts])
    return jnp.sum(jnp.where(chosen[None], pair[:, None, :], 0), axis=2)


def body(
    pre_query,
    pre_keys,
    pre_values,
    dec_query,
    dec_new_keys,
    dec_new_values,
    cache_keys,
    cache_values,
    cache_lens,
    pool_keys,
    pool_values,
    block_owner,
    block_count,
):
    table = block_table(block_owner[0, 0, :, 0], block_count[0, 0])
    lens = jnp.repeat(cache_lens[0], CACHE).reshape(ROWS // 16, 1, 16 * CACHE)
    bf16, f32 = jnp.bfloat16, jnp.float32
    anywhere = pl.BlockSpec(memory_space=pl.ANY)
    pre_out, dec_out, pages = pl.pallas_call(
        kernel,
        out_shape=(
            jax.ShapeDtypeStruct((1, SPAN_DEV, H * HD), bf16),
            jax.ShapeDtypeStruct((1, STEPS, ROWS, G * HD), bf16),
            jax.ShapeDtypeStruct((UNITS, 2 * CAP, BLOCK, HD), bf16),
        ),
        in_specs=[pl.BlockSpec(memory_space=pltpu.SMEM), pl.BlockSpec(memory_space=pltpu.VMEM)] + [anywhere] * 10,
        out_specs=(anywhere, anywhere, anywhere),
        scratch_shapes=[
            pltpu.VMEM((SPAN_DEV, H * HD), bf16),
            pltpu.VMEM((NTP, KEY_DEV, KVH * HD), bf16),
            pltpu.VMEM((NTP, KEY_DEV, KVH * HD), bf16),
            pltpu.VMEM((2, 32, BLOCK, KVH * HD), bf16),
            pltpu.VMEM((UNITS, 2 * CAP, BLOCK, HD), bf16),
            pltpu.VMEM((KVH, G * SPAN_DEV, HD), f32),
            pltpu.VMEM((KVH, G * SPAN_DEV, HD), f32),
            pltpu.VMEM((KVH, G * SPAN_DEV, HD), f32),
            pltpu.VMEM((SPAN_DEV, H * HD), bf16),
            pltpu.VMEM((STEPS, ROWS, G * HD), bf16),
            pltpu.VMEM((2, STEPS, ROWS, HD), bf16),
            pltpu.VMEM((2, ROWS, CACHE, HD), bf16),
            pltpu.VMEM((STEPS, ROWS, G * HD), bf16),
            pltpu.SemaphoreType.REGULAR,
            pltpu.SemaphoreType.DMA((8,)),
            pltpu.SemaphoreType.DMA((2,)),
            pltpu.SemaphoreType.DMA((2, 4)),
            pltpu.SemaphoreType.DMA((2, 4)),
            pltpu.SemaphoreType.DMA((2, 8)),
            pltpu.SemaphoreType.DMA,
            pltpu.SemaphoreType.DMA,
            pltpu.SemaphoreType.DMA((2,)),
        ],
        compiler_params=pltpu.CompilerParams(
            collective_id=0, has_side_effects=True, vmem_limit_bytes=56 * 2**20
        ),
    )(
        table,
        lens,
        pre_query,
        pre_keys,
        pre_values,
        dec_query,
        dec_new_keys,
        dec_new_values,
        cache_keys,
        cache_values,
        pool_keys,
        pool_values,
    )
    pages = pages.reshape(1, REPS, NTP, 2, CAP, BLOCK, HD)
    return pre_out, dec_out, pages[:, :, :, 0], pages[:, :, :, 1]


def solution(mesh):
    return jax.shard_map(
        body,
        mesh=mesh,
        in_specs=(
            P(("sec", "grp"), "tp", None),
            P(("sec", "grp"), "tp", None),
            P(("sec", "grp"), "tp", None),
            P(("sec", "grp"), None, None, "tp"),
            P(("sec", "grp"), None, None, "tp"),
            P(("sec", "grp"), None, None, "tp"),
            P(("sec", "grp"), None, None, "tp"),
            P(("sec", "grp"), None, None, "tp"),
            P(("sec", "grp"), None),
            P(("sec", "grp"), "tp", None, None, None),
            P(("sec", "grp"), "tp", None, None, None),
            P(("sec", "grp"), "tp", None, None),
            P(("sec", "grp"), "tp", None),
        ),
        out_specs=(
            P(("sec", "grp"), "tp", None),
            P(("sec", "grp"), None, None, "tp"),
            P(("sec", "grp"), None, None, None, None, "tp"),
            P(("sec", "grp"), None, None, None, None, "tp"),
        ),
        check_vma=False,
    )
```

time: 303 us -> 140 us (0.46); the launches traced: 298 us -> 140 us
  waiting for transfers between devices: 132 us -> 0 us
  Pallas kernels: 0 us -> 126 us
  matrix products: 60.8 us -> 0 us
  starting transfers between devices: 29.5 us -> 0 us
  local copies, waits for them, and re-layouts: 35.3 us -> 9.15 us
  other arithmetic: 26.4 us -> 4.28 us
  between operations: 14.3 us -> 0.65 us
    all_to_all x4 -> x0, waiting for transfers between devices: 131 us -> none  [the longest x1 47.4 us: handoff_part(): lax.all_to_all(send_values, ('sec', 'grp'), split_axis=0, concat_axis=0,...]
    pallas_call x0 -> x1, Pallas kernels: none -> 126 us  [body(): pl.pallas_call(kernel, out_shape=(jax.ShapeDtypeStruct((1, SPAN_DEV, H *...]
    dot_general x8 -> x0, matrix products: 60.8 us -> none  [the longest x1 30.5 us: update(): jnp.einsum('qkgt,tkd->qkgd', weights.astype(jnp.bfloat16), value_rows.res...]
    all_to_all x4 -> x0, starting transfers between devices: 29.5 us -> none  [the longest x1 11.2 us: handoff_part(): lax.all_to_all(send_keys, ('sec', 'grp'), split_axis=0, concat_axis=0, ti...]
    reduce_sum x4 -> x2, other arithmetic: 22.4 us -> 1.56 us  [the longest x1 0.91 us: block_table(): slot = jnp.sum(earlier.astype(jnp.int32), axis=1)]
    cond x5 -> x0, local copies, waits for them, and re-layouts: 11 us -> none
    unnamed x25 -> x7, local copies, waits for them, and re-layouts: 11.6 us -> 2.54 us
    squeeze x0 -> x1, local copies, waits for them, and re-layouts: none -> 5.77 us  [body(): return (pre_out, dec_out, pages[:, :, :, 0], pages[:, :, :, 1])]
  transfers between devices with their start and end apart: 6 -> 0, of which waited for: 4 -> 0; matrix products, arithmetic and copies ran while one was open for 9% -> 0% of each run, Pallas kernels for 0% -> 0%
where the time goes in v1:
time: 140 us
  Pallas kernels  126 us (90%)
  local copies, waits for them, and re-layouts  9.15 us (7%)
  other arithmetic  4.28 us (3%)
    pallas_call x1, Pallas kernels, body(): pl.pallas_call(kernel, out_shape=(jax.ShapeDtypeStruct((1, SPAN_DEV, H *...  126 us
    squeeze x1, local copies, waits for them, and re-layouts, body(): return (pre_out, dec_out, pages[:, :, :, 0], pages[:, :, :, 1])  5.77 us

profile of v1, /device:TPU:48, one launch (start us, length us, event | category | flops | bytes accessed | tf_op | source)
XLA Modules:
  0.0 140.2 jit_solution(2389966954599037637)
XLA Ops:
  0.6 0.5 broadcast.25
  1.1 1.3 reduce.3
  2.5 0.9 convert_reduce_fusion
  3.4 0.7 multiply_add_fusion
  4.0 0.7 pad_add_fusion
  4.7 0.1 broadcast_in_dim.36
  4.8 0.1 iota_compare_fusion
  4.9 0.7 select_reduce_fusion.table
  5.5 0.1 broadcast_in_dim.37
  5.6 0.7 broadcast_in_dim.38.lens
  6.3 126.1 %shard_map.156 = (bf16[1,128,8192]{2,1,0:T(8,128)(2,1)}, bf16[1,2,64,1024]{3,2,1,0:T(8,128)(2,1)}, bf16[256,4,16,128]{3,2,1,0:T(8,128)(2,1)}) custom-call(s32[2,64]{1,0:T(2,128)} %select_reduce_fusion.table, s32[4,1,256]{2,1,0:T(1,128)} %broadcast_in_dim.38.lens, bf16[1,128,8192]{2,1,0:T(8,128)(2,1)} %pre_q.1, bf16[1,256,1024]{2,1,0:T(8,128)(2,1)} %pre_k.1, ...), custom_call_target="tpu_custom_call" | custom-call | tf_op jit(solution)/shard_map/pallas_call | solution.py:375
  132.4 0.0 copy-start
  132.4 5.8 %slice_bitcast_fusion = (bf16[1,32,8,2,16,128]{5,4,3,2,1,0:T(8,128)(2,1)}, bf16[1,32,8,2,16,128]{5,4,3,2,1,0:T(8,128)(2,1)}) fusion(bf16[1,32,8,2,2,16,128]{6,5,4,3,2,1,0:T(8,128)(2,1)} %bitcast.12), kind=kLoop, calls=%fused_computation | loop fusion | bytes 8388608 | tf_op jit(solution)/shard_map/squeeze | solution.py:426
  138.2 0.0 copy-done
  138.2 0.0 copy-start.1
  138.2 1.3 copy.25
  139.5 0.0 copy-done.1
  139.5 0.7 copy.26
  (1 shorter events, 0.0 us)
Async XLA Ops:
  132.4 5.8 %copy-start = (bf16[1,128,8192]{2,1,0:T(8,128)(2,1)S(1)}, bf16[1,128,8192]{2,1,0:T(8,128)(2,1)}, u32[]{:S(2)}) copy-start(bf16[1,128,8192]{2,1,0:T(8,128)(2,1)} %get-tuple-element.16) | copy-start | bytes 6291460
  138.2 1.3 copy-start.1

commit v2 on v1

--- a/solution.py
+++ b/solution.py
@@ -37,7 +37,8 @@
 
 
 def kernel(
-    table,
+    owners,
+    counts,
     lens,
     pre_q,
     pre_k,
@@ -51,7 +52,8 @@
     pool_v,
     pre_out,
     dec_out,
-    pages,
+    pages_k,
+    pages_v,
     qbuf,
     kbuf,
     vbuf,
@@ -65,10 +67,15 @@
     nbuf,
     cbuf,
     dobuf,
+    lenbuf,
+    codebuf,
+    table,
     ready,
     load_sem,
+    table_sem,
     own_sem,
     kv_send,
+    kv_onward,
     kv_relay,
     kv_recv,
     page_send,
@@ -85,6 +92,8 @@
 
     def sibling(k):
         return lax.rem(tp + k, NTP)
+
+    pages = (pages_k, pages_v)
 
     loads = [
         pltpu.make_async_copy(pool_k.at[0, 0], poolbuf.at[0], load_sem.at[0]),
@@ -116,6 +125,45 @@
         copy.start()
     own_k.start()
     own_v.start()
+
+    pool_len = owners.shape[2]
+    first = lax.broadcasted_iota(jnp.int32, (pool_len, pool_len), 0)
+    second = lax.broadcasted_iota(jnp.int32, (pool_len, pool_len), 1)
+    same = first == second
+    owner_col = owners[0, 0]
+    owner_row = jnp.sum(jnp.where(same, owner_col, 0), axis=0, keepdims=True)
+    count_col = jnp.sum(jnp.where(same, counts[0], 0), axis=1, keepdims=True)
+    earlier = jnp.logical_and(owner_row == owner_col, second < first)
+    slot_col = jnp.sum(jnp.where(earlier, 1, 0), axis=1, keepdims=True)
+    chosen = owner_col * CAP + slot_col == lax.broadcasted_iota(jnp.int32, (pool_len, 128), 1)
+    block_col = lax.broadcasted_iota(jnp.int32, (pool_len, 128), 0)
+    codebuf[0:1] = jnp.sum(jnp.where(chosen, block_col, 0), axis=0, keepdims=True)
+    codebuf[1:2] = jnp.sum(jnp.where(chosen, count_col, 0), axis=0, keepdims=True)
+    to_scalars = pltpu.make_async_copy(codebuf, table, table_sem)
+    to_scalars.start()
+    first = lax.broadcasted_iota(jnp.int32, (ROWS, ROWS), 0)
+    second = lax.broadcasted_iota(jnp.int32, (ROWS, ROWS), 1)
+    len_col = jnp.sum(jnp.where(first == second, lens[...], 0), axis=1, keepdims=True)
+    lenbuf[...] = jnp.broadcast_to(len_col, lenbuf.shape)
+    to_scalars.wait()
+
+    loads[0].wait()
+    loads[1].wait()
+    token = lax.broadcasted_iota(jnp.int32, (BLOCK, KVH * HD), 0)
+
+    def pack(owner, _):
+        for slot in range(CAP):
+            block = table[0, owner * CAP + slot]
+            live = table[1, owner * CAP + slot]
+            keep = token < live
+            for kv in range(2):
+                rows = poolbuf[kv, block]
+                rows = jnp.where(keep, rows, jnp.zeros_like(rows))
+                for t in range(NTP):
+                    sendbuf[kv, owner * NTP + t, slot] = rows[:, t * HD : (t + 1) * HD]
+        return 0
+
+    lax.fori_loop(0, REPS, pack, 0)
     pl.semaphore_wait(barrier, REPS - 1 + NTP - 1)
 
     def vouch(k, _):
@@ -143,6 +191,23 @@
             device_id_type=MESH,
         )
 
+    def kv_forward(kv):
+        buf = (kbuf, vbuf)[kv]
+        source, target = (chip_at(2), chip_at(1)) if kv == 0 else (chip_at(1), chip_at(2))
+        chunk = source * 2 + core
+        return pltpu.make_async_remote_copy(
+            src_ref=buf.at[chunk],
+            dst_ref=buf.at[chunk],
+            send_sem=kv_onward.at[kv],
+            recv_sem=kv_recv.at[kv, chunk],
+            device_id=(sec, grp, target * 2 + core),
+            device_id_type=MESH,
+        )
+
+    def forwards(kv):
+        source, target = (chip_at(2), chip_at(1)) if kv == 0 else (chip_at(1), chip_at(2))
+        return jnp.logical_and(uses(source, y), uses(source, target))
+
     def kv_relayed(yy, kv):
         buf = (kbuf, vbuf)[kv]
         chunk = yy * 2 + core
@@ -159,50 +224,35 @@
         buf = (kbuf, vbuf)[kv]
         return pltpu.make_async_copy(buf.at[chunk], buf.at[chunk], kv_recv.at[kv, chunk])
 
-    for j in (1, 2, 3, 0):
+    for j in (1, 2, 0):
         @pl.when(uses(y, chip_at(j)))
         def _():
             kv_direct(j, 0).start()
             kv_direct(j, 1).start()
 
     pl.semaphore_wait(ready, NTP - 1)
-    loads[0].wait()
-    loads[1].wait()
-    token = lax.broadcasted_iota(jnp.int32, (BLOCK, KVH * HD), 0)
-
-    def pack(owner):
-        for slot in range(CAP):
-            block = table[0, owner * CAP + slot]
-            live = table[1, owner * CAP + slot]
-            keep = token < live
-            for kv in range(2):
-                rows = poolbuf[kv, block]
-                rows = jnp.where(keep, rows, jnp.zeros_like(rows))
-                for t in range(NTP):
-                    sendbuf[owner * NTP + t, kv * CAP + slot] = rows[:, t * HD : (t + 1) * HD]
-
-    def page_copy(s, g, t):
+
+    def page_copy(kv, s, g, t):
         return pltpu.make_async_remote_copy(
-            src_ref=sendbuf.at[(s * 16 + g) * NTP + t],
-            dst_ref=pages.at[me],
-            send_sem=page_send,
-            recv_sem=page_recv,
+            src_ref=sendbuf.at[kv, (s * 16 + g) * NTP + t],
+            dst_ref=pages[kv].at[me],
+            send_sem=page_send.at[kv],
+            recv_sem=page_recv.at[kv],
             device_id=(s, g, t),
             device_id_type=MESH,
         )
 
     def hand_off(k, _):
-        s, g = shifted(k)
-        pack(s * 16 + g)
-        for i in range(NTP):
-            page_copy(s, g, sibling(i)).start()
-        return 0
-
-    lax.fori_loop(1, REPS, hand_off, 0)
-    pack(sec * 16 + grp)
-    for i in range(1, NTP):
-        page_copy(sec, grp, sibling(i)).start()
-    pltpu.make_async_copy(sendbuf.at[me], pages.at[me], page_recv).start()
+        s, g = replica_at(lax.rem(x + lax.rem(k // 8, 4), 4), lax.rem(z + lax.rem(k, 8), 8))
+        t = lax.rem(y + k // 64, 4) * 2 + lax.rem(core + lax.rem(k // 32, 2), 2)
+        page_copy(0, s, g, t).start()
+        page_copy(1, s, g, t).start()
+        return 0
+
+    quarter = UNITS // 4
+    lax.fori_loop(1, quarter, hand_off, 0)
+    for kv in range(2):
+        pltpu.make_async_copy(sendbuf.at[kv, me], pages[kv].at[me], page_recv.at[kv]).start()
 
     for copy in loads[2:]:
         copy.wait()
@@ -228,7 +278,8 @@
         fresh_v = jnp.concatenate([nbuf[1, s, rows] for s in range(STEPS)], axis=0)
         s1 = lax.dot_general(query, res_k, over_d, preferred_element_type=jnp.float32)
         s2 = lax.dot_general(query, fresh_k, over_d, preferred_element_type=jnp.float32)
-        ok = jnp.logical_and(same_row, slot_of < lens[i])
+        live = jnp.concatenate([lenbuf[rows]] * (STEPS * G), axis=0)
+        ok = jnp.logical_and(same_row, slot_of < jnp.concatenate([live] * (16 * CACHE // HD), axis=1))
         s1 = jnp.where(ok, s1 * LOG2E_SCALE, MASKED)
         s2 = jnp.where(fresh_ok, s2 * LOG2E_SCALE, MASKED)
         peak = jnp.maximum(jnp.max(s1, axis=1, keepdims=True), jnp.max(s2, axis=1, keepdims=True))
@@ -257,8 +308,7 @@
     )
     ones = jnp.ones((CHIP_KEYS, HD), jnp.bfloat16)
 
-    def attend(yy):
-        reach = PRIOR + SPAN_DEV * tp - CHIP_KEYS * yy
+    def attend(yy, reach, masked):
         allowed = ahead <= reach
 
         def head(g, _):
@@ -266,9 +316,10 @@
             keys = kbuf[pl.ds(yy * 2, 2), :, lanes].reshape(CHIP_KEYS, HD)
             values = vbuf[pl.ds(yy * 2, 2), :, lanes].reshape(CHIP_KEYS, HD)
             values = jnp.concatenate([values, ones], axis=1)
-            for part in range(G * SPAN_DEV // ROW_TILE):
-                where = pl.ds(part * ROW_TILE, ROW_TILE)
-                heads = ROW_TILE // SPAN_DEV
+            parts = G * SPAN_DEV // ROW_TILE
+            heads = ROW_TILE // SPAN_DEV
+
+            def scores(part):
                 query = jnp.concatenate(
                     [
                         qbuf[:, pl.ds(pl.multiple_of((g * G + part * heads + h) * HD, HD), HD)]
@@ -276,16 +327,24 @@
                     ],
                     axis=0,
                 )
-                s = lax.dot_general(query, keys, over_d, preferred_element_type=jnp.float32)
-                s = jnp.where(allowed, s * LOG2E_SCALE, MASKED)
+                return lax.dot_general(query, keys, over_d, preferred_element_type=jnp.float32)
+
+            s = scores(0)
+            for part in range(parts):
+                following = scores(part + 1) if part + 1 < parts else None
+                where = pl.ds(part * ROW_TILE, ROW_TILE)
+                s = s * LOG2E_SCALE
+                if masked:
+                    s = jnp.where(allowed, s, MASKED)
                 old = top[g, where]
                 new = jnp.maximum(old, jnp.max(s, axis=1, keepdims=True))
+                weights = jnp.exp2(s - jnp.concatenate([new] * (CHIP_KEYS // HD), axis=1))
+                fade = jnp.exp2(old - new)
+                mix = jnp.dot(weights.astype(jnp.bfloat16), values, preferred_element_type=jnp.float32)
                 top[g, where] = new
-                weights = jnp.exp2(s - jnp.concatenate([new] * (CHIP_KEYS // HD), axis=1))
-                mix = jnp.dot(weights.astype(jnp.bfloat16), values, preferred_element_type=jnp.float32)
-                fade = jnp.exp2(old - new)
                 accum[g, where] = accum[g, where] * fade + mix[:, :HD]
                 total[g, where] = total[g, where] * fade + mix[:, HD:]
+                s = following
             return 0
 
         lax.fori_loop(0, KVH, head, 0)
@@ -293,21 +352,63 @@
     own_k.wait()
     own_v.wait()
 
+    def relay(j, kv):
+        kv_arrival(chip_at(j) * 2 + core, kv).wait()
+        kv_relayed(chip_at(j), kv).start()
+
     def step(j, _):
         here = chip_at(j)
-        later = chip_at(j + 1)
-
-        @pl.when(jnp.logical_and(j < 3, uses(later, y)))
-        def _():
-            for kv in range(2):
-                kv_arrival(later * 2 + core, kv).wait()
-                kv_relayed(later, kv).start()
+
+        @pl.when(j == 1)
+        def _():
+            lax.fori_loop(quarter, 2 * quarter, hand_off, 0)
+
+            @pl.when(uses(chip_at(2), y))
+            def _():
+                relay(2, 0)
+
+            @pl.when(forwards(0))
+            def _():
+                kv_forward(0).start()
+
+            @pl.when(uses(chip_at(1), y))
+            def _():
+                relay(1, 1)
+
+            @pl.when(forwards(1))
+            def _():
+                kv_forward(1).start()
+
+            @pl.when(uses(chip_at(1), y))
+            def _():
+                relay(1, 0)
+
+            @pl.when(uses(chip_at(2), y))
+            def _():
+                relay(2, 1)
+
+        @pl.when(j == 2)
+        def _():
+            lax.fori_loop(2 * quarter, 4 * quarter, hand_off, 0)
+
+        @pl.when(jnp.logical_and(j == 2, uses(chip_at(3), y)))
+        def _():
+            relay(3, 0)
+            relay(3, 1)
 
         @pl.when(uses(here, y))
         def _():
             for kv in range(2):
                 kv_arrival(here * 2 + 1 - core, kv).wait()
-            attend(here)
+            reach = PRIOR + SPAN_DEV * tp - CHIP_KEYS * here
+
+            @pl.when(reach < CHIP_KEYS - 1)
+            def _():
+                attend(here, reach, True)
+
+            @pl.when(reach >= CHIP_KEYS - 1)
+            def _():
+                attend(here, reach, False)
 
         return 0
 
@@ -324,11 +425,16 @@
     pre_store = pltpu.make_async_copy(obuf, pre_out.at[0], store_sem.at[1])
     pre_store.start()
 
-    for j in range(4):
+    for j in range(3):
         @pl.when(uses(y, chip_at(j)))
         def _():
             kv_direct(j, 0).wait_send()
             kv_direct(j, 1).wait_send()
+
+    for kv in range(2):
+        @pl.when(forwards(kv))
+        def _():
+            kv_forward(kv).wait_send()
 
     for j in range(1, 4):
         @pl.when(uses(chip_at(j), y))
@@ -339,18 +445,9 @@
     dec_store.wait()
     pre_store.wait()
     some = pl.ds(0, UNITS - 1)
-    pltpu.make_async_copy(sendbuf.at[some], sendbuf.at[some], page_send).wait()
-    pltpu.make_async_copy(pages, pages, page_recv).wait()
-
-
-def block_table(owners, counts):
-    blocks = jnp.arange(owners.shape[0], dtype=jnp.int32)
-    earlier = (owners[None, :] == owners[:, None]) & (blocks[None, :] < blocks[:, None])
-    slot = jnp.sum(earlier.astype(jnp.int32), axis=1)
-    place = owners * CAP + slot
-    chosen = place[None, :] == jnp.arange(REPS * CAP, dtype=jnp.int32)[:, None]
-    pair = jnp.stack([blocks, counts])
-    return jnp.sum(jnp.where(chosen[None], pair[:, None, :], 0), axis=2)
+    for kv in range(2):
+        pltpu.make_async_copy(sendbuf.at[kv, some], sendbuf.at[kv, some], page_send.at[kv]).wait()
+        pltpu.make_async_copy(pages[kv], pages[kv], page_recv.at[kv]).wait()
 
 
 def body(
@@ -368,25 +465,24 @@
     block_owner,
     block_count,
 ):
-    table = block_table(block_owner[0, 0, :, 0], block_count[0, 0])
-    lens = jnp.repeat(cache_lens[0], CACHE).reshape(ROWS // 16, 1, 16 * CACHE)
     bf16, f32 = jnp.bfloat16, jnp.float32
     anywhere = pl.BlockSpec(memory_space=pl.ANY)
-    pre_out, dec_out, pages = pl.pallas_call(
+    pre_out, dec_out, pages_keys, pages_values = pl.pallas_call(
         kernel,
         out_shape=(
             jax.ShapeDtypeStruct((1, SPAN_DEV, H * HD), bf16),
             jax.ShapeDtypeStruct((1, STEPS, ROWS, G * HD), bf16),
-            jax.ShapeDtypeStruct((UNITS, 2 * CAP, BLOCK, HD), bf16),
+            jax.ShapeDtypeStruct((UNITS, CAP, BLOCK, HD), bf16),
+            jax.ShapeDtypeStruct((UNITS, CAP, BLOCK, HD), bf16),
         ),
-        in_specs=[pl.BlockSpec(memory_space=pltpu.SMEM), pl.BlockSpec(memory_space=pltpu.VMEM)] + [anywhere] * 10,
-        out_specs=(anywhere, anywhere, anywhere),
+        in_specs=[pl.BlockSpec(memory_space=pltpu.VMEM)] * 3 + [anywhere] * 10,
+        out_specs=(anywhere,) * 4,
         scratch_shapes=[
             pltpu.VMEM((SPAN_DEV, H * HD), bf16),
             pltpu.VMEM((NTP, KEY_DEV, KVH * HD), bf16),
             pltpu.VMEM((NTP, KEY_DEV, KVH * HD), bf16),
             pltpu.VMEM((2, 32, BLOCK, KVH * HD), bf16),
-            pltpu.VMEM((UNITS, 2 * CAP, BLOCK, HD), bf16),
+            pltpu.VMEM((2, UNITS, CAP, BLOCK, HD), bf16),
             pltpu.VMEM((KVH, G * SPAN_DEV, HD), f32),
             pltpu.VMEM((KVH, G * SPAN_DEV, HD), f32),
             pltpu.VMEM((KVH, G * SPAN_DEV, HD), f32),
@@ -395,22 +491,28 @@
             pltpu.VMEM((2, STEPS, ROWS, HD), bf16),
             pltpu.VMEM((2, ROWS, CACHE, HD), bf16),
             pltpu.VMEM((STEPS, ROWS, G * HD), bf16),
+            pltpu.VMEM((ROWS, HD), jnp.int32),
+            pltpu.VMEM((2, HD), jnp.int32),
+            pltpu.SMEM((2, HD), jnp.int32),
             pltpu.SemaphoreType.REGULAR,
             pltpu.SemaphoreType.DMA((8,)),
+            pltpu.SemaphoreType.DMA,
+            pltpu.SemaphoreType.DMA((2,)),
+            pltpu.SemaphoreType.DMA((2, 3)),
             pltpu.SemaphoreType.DMA((2,)),
             pltpu.SemaphoreType.DMA((2, 4)),
-            pltpu.SemaphoreType.DMA((2, 4)),
             pltpu.SemaphoreType.DMA((2, 8)),
-            pltpu.SemaphoreType.DMA,
-            pltpu.SemaphoreType.DMA,
+            pltpu.SemaphoreType.DMA((2,)),
+            pltpu.SemaphoreType.DMA((2,)),
             pltpu.SemaphoreType.DMA((2,)),
         ],
         compiler_params=pltpu.CompilerParams(
             collective_id=0, has_side_effects=True, vmem_limit_bytes=56 * 2**20
         ),
     )(
-        table,
-        lens,
+        block_owner,
+        block_count,
+        cache_lens,
         pre_query,
         pre_keys,
         pre_values,
@@ -422,8 +524,8 @@
         pool_keys,
         pool_values,
     )
-    pages = pages.reshape(1, REPS, NTP, 2, CAP, BLOCK, HD)
-    return pre_out, dec_out, pages[:, :, :, 0], pages[:, :, :, 1]
+    shape = (1, REPS, NTP, CAP, BLOCK, HD)
+    return pre_out, dec_out, pages_keys.reshape(shape), pages_values.reshape(shape)
 
 
 def solution(mesh):

time: 140 us -> 118 us (0.84); the launches traced: 140 us -> 117 us
  Pallas kernels: 126 us -> 107 us
  other arithmetic: 4.28 us -> 0 us
    pallas_call x1, Pallas kernels: 126 us -> 107 us  [body(): pl.pallas_call(kernel, out_shape=(jax.ShapeDtypeStruct((1, SPAN_DEV, H *...]
    unnamed x7 -> x11, local copies, waits for them, and re-layouts: 2.54 us -> 8.96 us
    squeeze x1 -> x0, local copies, waits for them, and re-layouts: 5.77 us -> none  [body(): return (pre_out, dec_out, pages[:, :, :, 0], pages[:, :, :, 1])]
    reduce_sum x2 -> x0, other arithmetic: 1.56 us -> none  [the longest x1 0.91 us: block_table(): slot = jnp.sum(earlier.astype(jnp.int32), axis=1)]
where the time goes in v2:
time: 118 us; the launch traced here: 117 us
  Pallas kernels  107 us (91%)
  local copies, waits for them, and re-layouts  8.96 us (8%)
    pallas_call x1, Pallas kernels, body(): pl.pallas_call(kernel, out_shape=(jax.ShapeDtypeStruct((1, SPAN_DEV, H *...  107 us
    unnamed x11, local copies, waits for them, and re-layouts  8.96 us

profile of v2, /device:TPU:48, one launch (start us, length us, event | category | flops | bytes accessed | tf_op | source)
XLA Modules:
  0.0 116.6 jit_solution(16280751339431165161)
XLA Ops:
  0.6 1.3 %copy.17.owners = s32[1,1,32,1]{3,2,1,0:T(8,128)} copy(s32[1,1,32,1]{2,3,1,0:T(1,128)} %param.24) | data formatting | bytes 256 | tf_op args[11]
  2.0 106.9 %shard_map.156 = (bf16[1,128,8192]{2,1,0:T(8,128)(2,1)}, bf16[1,2,64,1024]{3,2,1,0:T(8,128)(2,1)}, bf16[256,2,16,128]{3,2,1,0:T(8,128)(2,1)}, bf16[256,2,16,128]{3,2,1,0:T(8,128)(2,1)}) custom-call(s32[1,1,32,1]{3,2,1,0:T(8,128)} %copy.17.owners, s32[1,1,32]{2,1,0:T(1,128)} %counts.1, s32[1,64]{1,0:T(1,128)} %lens.1, bf16[1,128,8192]{2,1,0:T(8,128)(2,1)} %pre_q.1, ...), custom_call_target="tpu_custom_call" | custom-call | tf_op jit(solution)/shard_map/pallas_call | solution.py:470
  108.9 0.0 copy-start.2
  108.9 0.0 copy-start.1
  108.9 3.2 %copy.22 = bf16[1,128,8192]{2,1,0:T(8,128)(2,1)} copy(bf16[1,128,8192]{2,1,0:T(8,128)(2,1)} %get-tuple-element.16) | data formatting | bytes 4194304
  112.2 0.0 copy-done.2
  112.2 0.7 copy.23
  112.9 0.0 copy-done.1
  112.9 0.0 copy-start
  112.9 1.3 %copy.24 = bf16[1,32,8,2,16,128]{5,4,3,2,1,0:T(8,128)(2,1)} copy(bf16[1,32,8,2,16,128]{5,4,3,2,1,0:T(8,128)(2,1)S(1)} %bitcast.3) | data formatting | bytes 4194304
  114.2 1.0 copy-done
  115.2 1.3 %copy.25 = bf16[1,32,8,2,16,128]{5,4,3,2,1,0:T(8,128)(2,1)} copy(bf16[1,32,8,2,16,128]{5,4,3,2,1,0:T(8,128)(2,1)S(1)} %bitcast.2) | data formatting | bytes 4194304
Async XLA Ops:
  108.9 3.3 %copy-start.2 = (bf16[1,2,64,1024]{3,2,1,0:T(8,128)(2,1)S(1)}, bf16[1,2,64,1024]{3,2,1,0:T(8,128)(2,1)}, u32[]{:S(2)}) copy-start(bf16[1,2,64,1024]{3,2,1,0:T(8,128)(2,1)} %get-tuple-element.17) | copy-start | bytes 786436
  108.9 4.0 %copy-start.1 = (bf16[256,2,16,128]{3,2,1,0:T(8,128)(2,1)S(1)}, bf16[256,2,16,128]{3,2,1,0:T(8,128)(2,1)}, u32[]{:S(2)}) copy-start(bf16[256,2,16,128]{3,2,1,0:T(8,128)(2,1)} %get-tuple-element.10) | copy-start | bytes 6291460
  112.9 2.3 %copy-start = (bf16[256,2,16,128]{3,2,1,0:T(8,128)(2,1)S(1)}, bf16[256,2,16,128]{3,2,1,0:T(8,128)(2,1)}, u32[]{:S(2)}) copy-start(bf16[256,2,16,128]{3,2,1,0:T(8,128)(2,1)} %get-tuple-element.11) | copy-start | bytes 6291460

commit v3 on v2

--- a/solution.py
+++ b/solution.py
@@ -62,11 +62,9 @@
     top,
     total,
     accum,
-    obuf,
     dqbuf,
     nbuf,
     cbuf,
-    dobuf,
     lenbuf,
     codebuf,
     table,
@@ -80,7 +78,6 @@
     kv_recv,
     page_send,
     page_recv,
-    store_sem,
 ):
     x, y, z, core = position()
     sec, grp, tp = lax.axis_index("sec"), lax.axis_index("grp"), lax.axis_index("tp")
@@ -108,31 +105,32 @@
     own_k = pltpu.make_async_copy(pre_k.at[0], kbuf.at[tp], own_sem.at[0])
     own_v = pltpu.make_async_copy(pre_v.at[0], vbuf.at[tp], own_sem.at[1])
 
-    barrier = pltpu.get_barrier_semaphore()
-
-    def greet_replicas(k, _):
-        s, g = shifted(k)
-        pl.semaphore_signal(barrier, inc=1, device_id=(s, g, tp), device_id_type=MESH)
-        return 0
-
-    def greet_siblings(k, _):
-        pl.semaphore_signal(barrier, inc=1, device_id=(sec, grp, sibling(k)), device_id_type=MESH)
-        return 0
-
-    lax.fori_loop(1, REPS, greet_replicas, 0)
-    lax.fori_loop(1, NTP, greet_siblings, 0)
     for copy in loads:
         copy.start()
     own_k.start()
     own_v.start()
 
-    pool_len = owners.shape[2]
+    barrier = pltpu.get_barrier_semaphore()
+
+    def greet_replicas(k, _):
+        s, g = shifted(k)
+        pl.semaphore_signal(barrier, inc=1, device_id=(s, g, tp), device_id_type=MESH)
+        return 0
+
+    def greet_siblings(k, _):
+        pl.semaphore_signal(barrier, inc=1, device_id=(sec, grp, sibling(k)), device_id_type=MESH)
+        return 0
+
+    lax.fori_loop(1, REPS, greet_replicas, 0)
+    lax.fori_loop(1, NTP, greet_siblings, 0)
+
+    pool_len = owners.shape[1]
     first = lax.broadcasted_iota(jnp.int32, (pool_len, pool_len), 0)
     second = lax.broadcasted_iota(jnp.int32, (pool_len, pool_len), 1)
     same = first == second
-    owner_col = owners[0, 0]
-    owner_row = jnp.sum(jnp.where(same, owner_col, 0), axis=0, keepdims=True)
-    count_col = jnp.sum(jnp.where(same, counts[0], 0), axis=1, keepdims=True)
+    owner_row = owners[...]
+    owner_col = jnp.sum(jnp.where(same, owner_row, 0), axis=1, keepdims=True)
+    count_col = jnp.sum(jnp.where(same, counts[...], 0), axis=1, keepdims=True)
     earlier = jnp.logical_and(owner_row == owner_col, second < first)
     slot_col = jnp.sum(jnp.where(earlier, 1, 0), axis=1, keepdims=True)
     chosen = owner_col * CAP + slot_col == lax.broadcasted_iota(jnp.int32, (pool_len, 128), 1)
@@ -149,7 +147,8 @@
 
     loads[0].wait()
     loads[1].wait()
-    token = lax.broadcasted_iota(jnp.int32, (BLOCK, KVH * HD), 0)
+    token = lax.broadcasted_iota(jnp.int32, (BLOCK, HD), 0)
+    blank = jnp.zeros((BLOCK, HD), jnp.bfloat16)
 
     def pack(owner, _):
         for slot in range(CAP):
@@ -158,9 +157,9 @@
             keep = token < live
             for kv in range(2):
                 rows = poolbuf[kv, block]
-                rows = jnp.where(keep, rows, jnp.zeros_like(rows))
                 for t in range(NTP):
-                    sendbuf[kv, owner * NTP + t, slot] = rows[:, t * HD : (t + 1) * HD]
+                    part = rows[:, t * HD : (t + 1) * HD]
+                    sendbuf[kv, owner * NTP + t, slot] = jnp.where(keep, part, blank)
         return 0
 
     lax.fori_loop(0, REPS, pack, 0)
@@ -230,7 +229,6 @@
             kv_direct(j, 0).start()
             kv_direct(j, 1).start()
 
-    pl.semaphore_wait(ready, NTP - 1)
 
     def page_copy(kv, s, g, t):
         return pltpu.make_async_remote_copy(
@@ -250,7 +248,9 @@
         return 0
 
     quarter = UNITS // 4
-    lax.fori_loop(1, quarter, hand_off, 0)
+    lax.fori_loop(1, REPS, hand_off, 0)
+    pl.semaphore_wait(ready, NTP - 1)
+    lax.fori_loop(REPS, quarter, hand_off, 0)
     for kv in range(2):
         pltpu.make_async_copy(sendbuf.at[kv, me], pages[kv].at[me], page_recv.at[kv]).start()
 
@@ -292,12 +292,10 @@
         for s in range(STEPS):
             for h in range(G):
                 part = (s * G + h) * 16
-                dobuf[s, rows, h * HD : (h + 1) * HD] = out[part : part + 16]
+                dec_out[0, s, rows, h * HD : (h + 1) * HD] = out[part : part + 16]
         return 0
 
     lax.fori_loop(0, ROWS // 16, decode, 0)
-    dec_store = pltpu.make_async_copy(dobuf, dec_out.at[0], store_sem.at[0])
-    dec_store.start()
 
     top[...] = jnp.full_like(top, MASKED)
     total[...] = jnp.zeros_like(total)
@@ -387,9 +385,7 @@
             def _():
                 relay(2, 1)
 
-        @pl.when(j == 2)
-        def _():
-            lax.fori_loop(2 * quarter, 4 * quarter, hand_off, 0)
+            lax.fori_loop(2 * quarter, UNITS, hand_off, 0)
 
         @pl.when(jnp.logical_and(j == 2, uses(chip_at(3), y)))
         def _():
@@ -418,12 +414,10 @@
         for h in range(G):
             where = pl.ds(h * SPAN_DEV, SPAN_DEV)
             lanes = pl.ds(pl.multiple_of((g * G + h) * HD, HD), HD)
-            obuf[:, lanes] = (accum[g, where] / total[g, where]).astype(jnp.bfloat16)
+            pre_out[0, :, lanes] = (accum[g, where] / total[g, where]).astype(jnp.bfloat16)
         return 0
 
     lax.fori_loop(0, KVH, finish, 0)
-    pre_store = pltpu.make_async_copy(obuf, pre_out.at[0], store_sem.at[1])
-    pre_store.start()
 
     for j in range(3):
         @pl.when(uses(y, chip_at(j)))
@@ -442,12 +436,19 @@
             kv_relayed(chip_at(j), 0).wait_send()
             kv_relayed(chip_at(j), 1).wait_send()
 
-    dec_store.wait()
-    pre_store.wait()
     some = pl.ds(0, UNITS - 1)
     for kv in range(2):
         pltpu.make_async_copy(sendbuf.at[kv, some], sendbuf.at[kv, some], page_send.at[kv]).wait()
         pltpu.make_async_copy(pages[kv], pages[kv], page_recv.at[kv]).wait()
+
+
+def hand_on(*refs):
+    held, results, sems = refs[:4], refs[4:8], refs[8]
+    copies = [pltpu.make_async_copy(held[i], results[i], sems.at[i]) for i in range(4)]
+    for copy in copies:
+        copy.start()
+    for copy in copies:
+        copy.wait()
 
 
 def body(
@@ -466,17 +467,18 @@
     block_count,
 ):
     bf16, f32 = jnp.bfloat16, jnp.float32
-    anywhere = pl.BlockSpec(memory_space=pl.ANY)
+    outside = pl.BlockSpec(memory_space=pltpu.HBM)
+    on_chip = pl.BlockSpec(memory_space=pltpu.VMEM)
     pre_out, dec_out, pages_keys, pages_values = pl.pallas_call(
         kernel,
         out_shape=(
-            jax.ShapeDtypeStruct((1, SPAN_DEV, H * HD), bf16),
-            jax.ShapeDtypeStruct((1, STEPS, ROWS, G * HD), bf16),
-            jax.ShapeDtypeStruct((UNITS, CAP, BLOCK, HD), bf16),
-            jax.ShapeDtypeStruct((UNITS, CAP, BLOCK, HD), bf16),
+            pltpu.VMEM((1, SPAN_DEV, H * HD), bf16),
+            pltpu.VMEM((1, STEPS, ROWS, G * HD), bf16),
+            pltpu.VMEM((UNITS, CAP, BLOCK, HD), bf16),
+            pltpu.VMEM((UNITS, CAP, BLOCK, HD), bf16),
         ),
-        in_specs=[pl.BlockSpec(memory_space=pltpu.VMEM)] * 3 + [anywhere] * 10,
-        out_specs=(anywhere,) * 4,
+        in_specs=[on_chip] * 3 + [outside] * 10,
+        out_specs=(on_chip,) * 4,
         scratch_shapes=[
             pltpu.VMEM((SPAN_DEV, H * HD), bf16),
             pltpu.VMEM((NTP, KEY_DEV, KVH * HD), bf16),
@@ -486,11 +488,9 @@
             pltpu.VMEM((KVH, G * SPAN_DEV, HD), f32),
             pltpu.VMEM((KVH, G * SPAN_DEV, HD), f32),
             pltpu.VMEM((KVH, G * SPAN_DEV, HD), f32),
-            pltpu.VMEM((SPAN_DEV, H * HD), bf16),
             pltpu.VMEM((STEPS, ROWS, G * HD), bf16),
             pltpu.VMEM((2, STEPS, ROWS, HD), bf16),
             pltpu.VMEM((2, ROWS, CACHE, HD), bf16),
-            pltpu.VMEM((STEPS, ROWS, G * HD), bf16),
             pltpu.VMEM((ROWS, HD), jnp.int32),
             pltpu.VMEM((2, HD), jnp.int32),
             pltpu.SMEM((2, HD), jnp.int32),
@@ -504,14 +504,13 @@
             pltpu.SemaphoreType.DMA((2, 8)),
             pltpu.SemaphoreType.DMA((2,)),
             pltpu.SemaphoreType.DMA((2,)),
-            pltpu.SemaphoreType.DMA((2,)),
         ],
         compiler_params=pltpu.CompilerParams(
-            collective_id=0, has_side_effects=True, vmem_limit_bytes=56 * 2**20
+            collective_id=0, has_side_effects=True, vmem_limit_bytes=48 * 2**20
         ),
     )(
-        block_owner,
-        block_count,
+        block_owner.reshape(1, -1),
+        block_count.reshape(1, -1),
         cache_lens,
         pre_query,
         pre_keys,
@@ -524,6 +523,15 @@
         pool_keys,
         pool_values,
     )
+    results = (pre_out, dec_out, pages_keys, pages_values)
+    pre_out, dec_out, pages_keys, pages_values = pl.pallas_call(
+        hand_on,
+        out_shape=tuple(jax.ShapeDtypeStruct(v.shape, v.dtype) for v in results),
+        in_specs=[on_chip] * 4,
+        out_specs=(outside,) * 4,
+        scratch_shapes=[pltpu.SemaphoreType.DMA((4,))],
+        compiler_params=pltpu.CompilerParams(vmem_limit_bytes=2**20),
+    )(*results)
     shape = (1, REPS, NTP, CAP, BLOCK, HD)
     return pre_out, dec_out, pages_keys.reshape(shape), pages_values.reshape(shape)
 

time: 118 us -> 110 us (0.932)
  local copies, waits for them, and re-layouts: 8.96 us -> 0 us
  Pallas kernels: 107 us -> 109 us
    unnamed x11 -> x0, local copies, waits for them, and re-layouts: 8.96 us -> none
    pallas_call x1 -> x2, Pallas kernels: 107 us -> 109 us  [the longest x1 106 us: body(): pl.pallas_call(kernel, out_shape=(pltpu.VMEM((1, SPAN_DEV, H * HD), bf16)...]
where the time goes in v3:
time: 110 us; the launch traced here: 109 us
  Pallas kernels  109 us (99%)
    pallas_call x1, Pallas kernels, body(): pl.pallas_call(kernel, out_shape=(pltpu.VMEM((1, SPAN_DEV, H * HD), bf16)...  106 us
    pallas_call x1, Pallas kernels, body(): pl.pallas_call(hand_on, out_shape=tuple((jax.ShapeDtypeStruct(v.shape, v....  2.82 us

profile of v3, /device:TPU:48, one launch (start us, length us, event | category | flops | bytes accessed | tf_op | source)
XLA Modules:
  0.0 109.4 jit_solution(1595192568455756204)
XLA Ops:
  0.6 105.9 %shard_map.156 = (bf16[1,128,8192]{2,1,0:T(8,128)(2,1)S(1)}, bf16[1,2,64,1024]{3,2,1,0:T(8,128)(2,1)S(1)}, bf16[256,2,16,128]{3,2,1,0:T(8,128)(2,1)S(1)}, bf16[256,2,16,128]{3,2,1,0:T(8,128)(2,1)S(1)}) custom-call(s32[1,32]{1,0:T(1,128)} %bitcast.4, s32[1,32]{1,0:T(1,128)} %bitcast.5, s32[1,64]{1,0:T(1,128)} %lens.1, bf16[1,128,8192]{2,1,0:T(8,128)(2,1)} %pre_q.1, ...), custom_call_target="tpu_custom_call" | custom-call | tf_op jit(solution)/shard_map/pallas_call | solution.py:472
  106.6 2.8 %shard_map.157 = (bf16[1,128,8192]{2,1,0:T(8,128)(2,1)}, bf16[1,2,64,1024]{3,2,1,0:T(8,128)(2,1)}, bf16[256,2,16,128]{3,2,1,0:T(8,128)(2,1)}, bf16[256,2,16,128]{3,2,1,0:T(8,128)(2,1)}) custom-call(bf16[1,128,8192]{2,1,0:T(8,128)(2,1)S(1)} %get-tuple-element.12.refs_0_, bf16[1,2,64,1024]{3,2,1,0:T(8,128)(2,1)S(1)} %get-tuple-element.13.refs_1_, ...), custom_call_target="tpu_custom_call" | custom-call | tf_op jit(solution)/shard_map/pallas_call | solution.py:527

commit v4 on v3

--- a/solution.py
+++ b/solution.py
@@ -105,24 +105,26 @@
     own_k = pltpu.make_async_copy(pre_k.at[0], kbuf.at[tp], own_sem.at[0])
     own_v = pltpu.make_async_copy(pre_v.at[0], vbuf.at[tp], own_sem.at[1])
 
-    for copy in loads:
+    loads[0].start()
+    loads[1].start()
+
+    barrier = pltpu.get_barrier_semaphore()
+
+    def greet_replicas(k, _):
+        s, g = shifted(k)
+        pl.semaphore_signal(barrier, inc=1, device_id=(s, g, tp), device_id_type=MESH)
+        return 0
+
+    def greet_siblings(k, _):
+        pl.semaphore_signal(barrier, inc=1, device_id=(sec, grp, sibling(k)), device_id_type=MESH)
+        return 0
+
+    lax.fori_loop(1, REPS, greet_replicas, 0, unroll=True)
+    lax.fori_loop(1, NTP, greet_siblings, 0, unroll=True)
+    for copy in loads[2:]:
         copy.start()
     own_k.start()
     own_v.start()
-
-    barrier = pltpu.get_barrier_semaphore()
-
-    def greet_replicas(k, _):
-        s, g = shifted(k)
-        pl.semaphore_signal(barrier, inc=1, device_id=(s, g, tp), device_id_type=MESH)
-        return 0
-
-    def greet_siblings(k, _):
-        pl.semaphore_signal(barrier, inc=1, device_id=(sec, grp, sibling(k)), device_id_type=MESH)
-        return 0
-
-    lax.fori_loop(1, REPS, greet_replicas, 0)
-    lax.fori_loop(1, NTP, greet_siblings, 0)
 
     pool_len = owners.shape[1]
     first = lax.broadcasted_iota(jnp.int32, (pool_len, pool_len), 0)
@@ -150,7 +152,7 @@
     token = lax.broadcasted_iota(jnp.int32, (BLOCK, HD), 0)
     blank = jnp.zeros((BLOCK, HD), jnp.bfloat16)
 
-    def pack(owner, _):
+    def pack(owner):
         for slot in range(CAP):
             block = table[0, owner * CAP + slot]
             live = table[1, owner * CAP + slot]
@@ -160,9 +162,17 @@
                 for t in range(NTP):
                     part = rows[:, t * HD : (t + 1) * HD]
                     sendbuf[kv, owner * NTP + t, slot] = jnp.where(keep, part, blank)
-        return 0
-
-    lax.fori_loop(0, REPS, pack, 0)
+
+    def pack_group(group):
+        xx = lax.rem(x + group, 4)
+
+        def one(zz, _):
+            pack((zz // 4) * 16 + xx * 4 + lax.rem(zz, 4))
+            return 0
+
+        lax.fori_loop(0, 8, one, 0)
+
+    pack_group(0)
     pl.semaphore_wait(barrier, REPS - 1 + NTP - 1)
 
     def vouch(k, _):
@@ -240,17 +250,37 @@
             device_id_type=MESH,
         )
 
-    def hand_off(k, _):
-        s, g = replica_at(lax.rem(x + lax.rem(k // 8, 4), 4), lax.rem(z + lax.rem(k, 8), 8))
-        t = lax.rem(y + k // 64, 4) * 2 + lax.rem(core + lax.rem(k // 32, 2), 2)
-        page_copy(0, s, g, t).start()
-        page_copy(1, s, g, t).start()
-        return 0
-
-    quarter = UNITS // 4
-    lax.fori_loop(1, REPS, hand_off, 0)
+    def hand_off(group, first=0):
+        xx = lax.rem(x + lax.rem(group, 4), 4)
+        t = lax.rem(y + group // 8, 4) * 2 + lax.rem(core + lax.rem(group // 4, 2), 2)
+        for dz in range(first, 8):
+            s, g = replica_at(xx, lax.rem(z + dz, 8))
+            page_copy(0, s, g, t).start()
+            page_copy(1, s, g, t).start()
+
+    def cross(turn, _):
+        way = lax.rem(turn, 3)
+        dy = jnp.where(way == 0, 1, jnp.where(way == 1, 3, 2))
+        hand_off(dy * 8 + turn // 3)
+        return 0
+
+    def hand_off_groups(begin, end):
+        def one(group, _):
+            hand_off(group)
+            return 0
+
+        lax.fori_loop(begin, end, one, 0)
+
+    hand_off(0, 1)
+
+    def first_round(group, _):
+        pack_group(group)
+        hand_off(group)
+        return 0
+
+    lax.fori_loop(1, 4, first_round, 0)
     pl.semaphore_wait(ready, NTP - 1)
-    lax.fori_loop(REPS, quarter, hand_off, 0)
+    hand_off_groups(4, 8)
     for kv in range(2):
         pltpu.make_async_copy(sendbuf.at[kv, me], pages[kv].at[me], page_recv.at[kv]).start()
 
@@ -359,7 +389,7 @@
 
         @pl.when(j == 1)
         def _():
-            lax.fori_loop(quarter, 2 * quarter, hand_off, 0)
+            lax.fori_loop(0, 8, cross, 0)
 
             @pl.when(uses(chip_at(2), y))
             def _():
@@ -385,7 +415,7 @@
             def _():
                 relay(2, 1)
 
-            lax.fori_loop(2 * quarter, UNITS, hand_off, 0)
+            lax.fori_loop(8, 24, cross, 0)
 
         @pl.when(jnp.logical_and(j == 2, uses(chip_at(3), y)))
         def _():
@@ -444,7 +474,12 @@
 
 def hand_on(*refs):
     held, results, sems = refs[:4], refs[4:8], refs[8]
-    copies = [pltpu.make_async_copy(held[i], results[i], sems.at[i]) for i in range(4)]
+    pieces = [(0, 1, pl.ds(i * 32, 32)) for i in range(4)]
+    pieces += [(ref, 0, pl.ds(i * 64, 64)) for ref in (2, 3) for i in range(4)]
+    copies = [pltpu.make_async_copy(held[1], results[1], sems.at[0])]
+    for i, (ref, axis, part) in enumerate(pieces):
+        where = (0, part) if axis else (part,)
+        copies.append(pltpu.make_async_copy(held[ref].at[where], results[ref].at[where], sems.at[i + 1]))
     for copy in copies:
         copy.start()
     for copy in copies:
@@ -529,7 +564,7 @@
         out_shape=tuple(jax.ShapeDtypeStruct(v.shape, v.dtype) for v in results),
         in_specs=[on_chip] * 4,
         out_specs=(outside,) * 4,
-        scratch_shapes=[pltpu.SemaphoreType.DMA((4,))],
+        scratch_shapes=[pltpu.SemaphoreType.DMA((13,))],
         compiler_params=pltpu.CompilerParams(vmem_limit_bytes=2**20),
     )(*results)
     shape = (1, REPS, NTP, CAP, BLOCK, HD)

time: 110 us -> 109 us (level)
  the two profiles are of different devices: /device:TPU:48 before, /device:TPU:1 now
where the time goes in v4:
time: 109 us
  Pallas kernels  109 us (100%)
    pallas_call x1, Pallas kernels, body(): pl.pallas_call(kernel, out_shape=(pltpu.VMEM((1, SPAN_DEV, H * HD), bf16)...  106 us
    pallas_call x1, Pallas kernels, body(): pl.pallas_call(hand_on, out_shape=tuple((jax.ShapeDtypeStruct(v.shape, v....  2.85 us

profile of v4, /device:TPU:1, one launch (start us, length us, event | category | flops | bytes accessed | tf_op | source)
XLA Modules:
  0.0 109.3 jit_solution(17416966574238204874)
XLA Ops:
  0.6 105.9 %shard_map.156 = (bf16[1,128,8192]{2,1,0:T(8,128)(2,1)S(1)}, bf16[1,2,64,1024]{3,2,1,0:T(8,128)(2,1)S(1)}, bf16[256,2,16,128]{3,2,1,0:T(8,128)(2,1)S(1)}, bf16[256,2,16,128]{3,2,1,0:T(8,128)(2,1)S(1)}) custom-call(s32[1,32]{1,0:T(1,128)} %bitcast.4, s32[1,32]{1,0:T(1,128)} %bitcast.5, s32[1,64]{1,0:T(1,128)} %lens.1, bf16[1,128,8192]{2,1,0:T(8,128)(2,1)} %pre_q.1, ...), custom_call_target="tpu_custom_call" | custom-call | tf_op jit(solution)/shard_map/pallas_call | solution.py:507
  106.5 2.8 %shard_map.157 = (bf16[1,128,8192]{2,1,0:T(8,128)(2,1)}, bf16[1,2,64,1024]{3,2,1,0:T(8,128)(2,1)}, bf16[256,2,16,128]{3,2,1,0:T(8,128)(2,1)}, bf16[256,2,16,128]{3,2,1,0:T(8,128)(2,1)}) custom-call(bf16[1,128,8192]{2,1,0:T(8,128)(2,1)S(1)} %get-tuple-element.12.refs_0_, bf16[1,2,64,1024]{3,2,1,0:T(8,128)(2,1)S(1)} %get-tuple-element.13.refs_1_, ...), custom_call_target="tpu_custom_call" | custom-call | tf_op jit(solution)/shard_map/pallas_call | solution.py:562
